TPU v7x, 128 devices: a whole 4x4x4 slice. The times are simulated.
128 devices in a mesh: rows: 2 (over core), cols: 64 (over z, y, x).
Axes of the slice: x: 4, y: 4, z: 4, core: 2. Of those that a mesh axis runs over, the one named last changes fastest.
Arguments:
- row_geom: float32 [3072, 8, 1024], P('cols', None, 'rows'), may hold values from -1 to 1
- col_geom: float32 [3072, 8, 1024], P('cols', None, 'rows'), may hold values from -1 to 1
- row_start: int32 [3072], P('cols'), may hold values from 1024 to 397951
- col_start: int32 [3072], P('cols'), may hold values from 512 to 398463, as said below
- block_count: int32 [64], P('cols'), may hold values from 1 to 48, 768 in all
- sketch: float32 [1024, 64], replicated, may hold values from -0.75 to 0.75
Outputs:
- left_factor: float32 [3072, 64, 1024], P('cols', None, 'rows')
- right_factor: float32 [3072, 64, 1024], P('cols', None, 'rows')
Inputs may be any that keep to these rules, and one draw needn't show every extreme that they name: `block_count`: each owner's counts are at most 48; all counts together sum to exactly 48 // 4 times the number of owners. Places beyond an owner's count are unused. col_start minus row_start lies between -512 and 512.
All inputs are finite; a program needn't handle non-finite values. No bound on the sum of `block_count` on one device may be relied on, other than what follows from the above.
Results may differ from a plain program's by a relative error of at most 0.0003.
Values sent between devices are 32-bit elements; how exact they have to be, the bound alone decides.
A program may use at most 128 MiB of HBM per device.

v0:
```python
import jax
import jax.numpy as jnp
from jax import lax
from jax.sharding import PartitionSpec as P

HIGHEST = lax.Precision.HIGHEST


def copy_for_each(shard, axis):
    copies = jnp.broadcast_to(shard, (lax.axis_size(axis), *shard.shape))
    return lax.all_to_all(copies, axis, split_axis=0, concat_axis=0, tiled=True)


def combined_pairwise(pieces, combine):
    while len(jax.tree.leaves(pieces)[0]) > 1:
        pieces = jax.vmap(combine)(*(pieces[side::2] for side in (0, 1)))
    return pieces[0]


def carried_in(shard, axis, combine, identity):
    count, here = (lax.axis_size(axis), lax.axis_index(axis))
    passed = jnp.arange(count) < here

    def kept(part, zero, own):
        part = jnp.where(
            passed.reshape(-1, *(1 for _ in own.shape)), part, jnp.asarray(zero, own.dtype)
        )
        return part

    pieces = copy_for_each(shard, axis)
    return combined_pairwise(kept(pieces, identity, shard), combine)


def kernel_block(row_geo, col_geo, start_row, start_col):
    sep_x = row_geo[:, 0, :, None] - col_geo[:, 0, None, :]
    sep_y = row_geo[:, 1, :, None] - col_geo[:, 1, None, :]
    sep_z = row_geo[:, 2, :, None] - col_geo[:, 2, None, :]
    row_area = 0.1 + 0.05 * row_geo[:, 6, :, None]
    col_area = 0.1 + 0.05 * col_geo[:, 6, None, :]
    inverse = 1.0 / (sep_x * sep_x + sep_y * sep_y + sep_z * sep_z + row_area + col_area)
    normal_dot = (
        row_geo[:, 3, :, None] * col_geo[:, 3, None, :]
        + row_geo[:, 4, :, None] * col_geo[:, 4, None, :]
        + row_geo[:, 5, :, None] * col_geo[:, 5, None, :]
    )
    row_proj = (
        row_geo[:, 3, :, None] * sep_x
        + row_geo[:, 4, :, None] * sep_y
        + row_geo[:, 5, :, None] * sep_z
    )
    col_proj = (
        col_geo[:, 3, None, :] * sep_x
        + col_geo[:, 4, None, :] * sep_y
        + col_geo[:, 5, None, :] * sep_z
    )
    influence = (
        col_area * (normal_dot - 3.0 * row_proj * col_proj * inverse) * inverse * jnp.sqrt(inverse)
    )
    self_term = 4.0 + 2.0 * row_geo[:, 7, :, None]
    row_ids = jnp.arange(row_geo.shape[2], dtype=jnp.int32)[:, None]
    col_ids = jnp.arange(col_geo.shape[2], dtype=jnp.int32)[None, :]
    distance = (start_row - start_col)[:, None, None]
    match = (col_ids - row_ids)[None, :, :] == distance
    return jnp.where(match, self_term, influence)


def factor_pair(gram, projected):
    rank = gram.shape[1]
    trace = jnp.trace(gram, axis1=1, axis2=2)
    ridge = 0.01 * trace / rank + 0.001
    system = gram + ridge[:, None, None] * jnp.eye(rank, dtype=gram.dtype)[None]
    lower = jnp.linalg.cholesky(system)
    half = lax.linalg.triangular_solve(lower, projected, left_side=True, lower=True)
    return lax.linalg.triangular_solve(lower, half, left_side=True, lower=True, transpose_a=True)


def pick_group(total, most):
    group = most
    while total % group:
        group -= 1
    return group


def add_counts(earlier, later):
    return earlier + later


def whole_compress(row_geo, col_geo, row_start, col_start, sketch):
    slots, geo_count, width = row_geo.shape
    rank = sketch.shape[1]
    ranks = lax.axis_size("rows")
    my_index = lax.axis_index("rows")
    turns = slots // ranks
    stacked = jnp.stack([row_geo, col_geo], 1).reshape(turns, ranks, 2, geo_count, width)
    gathered = lax.all_to_all(stacked, "rows", split_axis=1, concat_axis=4, tiled=True)
    full_width = gathered.shape[4]
    full_rows = gathered[:, 0, 0]
    full_cols = gathered[:, 0, 1]
    my_row_start = lax.dynamic_index_in_dim(
        row_start.reshape(turns, ranks), my_index, 1, keepdims=False
    )
    my_col_start = lax.dynamic_index_in_dim(
        col_start.reshape(turns, ranks), my_index, 1, keepdims=False
    )
    group = pick_group(turns, 2)
    batches = turns // group

    def step(carry, packed):
        rows_part, cols_part, first_row, first_col = packed
        block = kernel_block(rows_part, cols_part, first_row, first_col)
        sketched = jnp.einsum("gik,kr->gir", block, sketch, precision=HIGHEST)
        gram = jnp.einsum("gir,gis->grs", sketched, sketched, precision=HIGHEST)
        projected = jnp.einsum("gik,gir->grk", block, sketched, precision=HIGHEST)
        right = factor_pair(gram, projected)
        left = jnp.transpose(sketched, (0, 2, 1))
        return (carry, jnp.stack([left, right], 1))

    packed = (
        full_rows.reshape(batches, group, geo_count, full_width),
        full_cols.reshape(batches, group, geo_count, full_width),
        my_row_start.reshape(batches, group),
        my_col_start.reshape(batches, group),
    )
    results = lax.scan(step, jnp.int32(0), packed)[1]
    results = results.reshape(turns, 1, 2, rank, full_width)
    returned = lax.all_to_all(results, "rows", split_axis=4, concat_axis=1, tiled=True)
    flat = returned.reshape(slots, 2, rank, width)
    return (flat[:, 0], flat[:, 1])


def compress(row_geo, col_geo, row_start, col_start, sketch):
    return whole_compress(row_geo, col_geo, row_start, col_start, sketch)


def on_device(row_geom, col_geom, row_start, col_start, block_count, sketch):
    owned, geo_count, width = row_geom.shape
    rank = sketch.shape[1]
    count = block_count[0]
    order = jnp.arange(owned, dtype=jnp.int32)
    owners = lax.axis_size("cols")
    capacity = -(-owned // owners)
    total_slots = owners * capacity
    start = carried_in(count, "cols", add_counts, jnp.int32(0))
    workers = jnp.arange(owners, dtype=jnp.int32)[:, None]
    places = jnp.arange(capacity, dtype=jnp.int32)[None, :]
    picked = places * owners + (workers - start) % owners
    is_sent = picked < count
    safe = jnp.minimum(picked, owned - 1)
    send_rows = jnp.where(is_sent[:, :, None, None], row_geom[safe], 0.0)
    send_cols = jnp.where(is_sent[:, :, None, None], col_geom[safe], 0.0)
    send_ranges = jnp.stack(
        [
            jnp.where(is_sent, row_start[safe], 0),
            jnp.where(is_sent, col_start[safe], 0),
            jnp.where(is_sent, start + picked, -1),
        ],
        2,
    ).astype(jnp.float32)
    got_rows, got_cols, got_ranges = (
        lax.all_to_all(send_rows, "cols", split_axis=0, concat_axis=0, tiled=True),
        lax.all_to_all(send_cols, "cols", split_axis=0, concat_axis=0, tiled=True),
        lax.all_to_all(send_ranges, "cols", split_axis=0, concat_axis=0, tiled=True),
    )
    ranges = got_ranges.reshape(total_slots, 3).astype(jnp.int32)
    busy = owned // 4
    flat_ids = ranges[:, 2]
    is_live = flat_ids >= 0
    target = jnp.where(is_live, flat_ids // owners, busy)
    chosen = target[None, :] == jnp.arange(busy, dtype=jnp.int32)[:, None]
    source = jnp.sum(
        jnp.where(chosen, jnp.arange(total_slots, dtype=jnp.int32)[None, :], 0), axis=1
    )
    busy_rows = got_rows.reshape(total_slots, geo_count, width)[source]
    busy_cols = got_cols.reshape(total_slots, geo_count, width)[source]
    left_busy, right_busy = compress(
        busy_rows, busy_cols, ranges[source, 0], ranges[source, 1], sketch
    )
    slot_pick = jnp.minimum(target, busy - 1)
    back_left = jnp.where(is_live[:, None, None], left_busy[slot_pick], 0.0).reshape(
        owners, capacity, rank, width
    )
    back_right = jnp.where(is_live[:, None, None], right_busy[slot_pick], 0.0).reshape(
        owners, capacity, rank, width
    )
    returned_left, returned_right = (
        lax.all_to_all(back_left, "cols", split_axis=0, concat_axis=0, tiled=True),
        lax.all_to_all(back_right, "cols", split_axis=0, concat_axis=0, tiled=True),
    )
    flat_index = (start + order) % owners * capacity + order // owners
    left = returned_left.reshape(total_slots, rank, width)[flat_index]
    right = returned_right.reshape(total_slots, rank, width)[flat_index]
    is_kept = (order < count)[:, None, None]
    return (jnp.where(is_kept, left, 0.0), jnp.where(is_kept, right, 0.0))


def solution(mesh):
    placed = (
        P("cols", None, "rows"),
        P("cols", None, "rows"),
        P("cols"),
        P("cols"),
        P("cols"),
        P(),
    )
    return jax.shard_map(
        on_device,
        mesh=mesh,
        in_specs=placed,
        out_specs=(P("cols", None, "rows"), P("cols", None, "rows")),
        check_vma=False,
    )
```

profile of v0, /device:TPU:4, one launch (start us, length us, event | category | flops | bytes accessed | tf_op | source)
XLA Modules:
  0.0 634.6 jit_solution(12272790962720469400)
XLA Ops:
  2.0 11.5 %all-to-all-start = ((s32[64,1,1]{2,1,0:T(1,128)}), s32[64,1,1]{2,1,0:T(1,128)S(1)}, u32[]{:S(2)}, u32[]{:S(2)}) async-start(s32[64,1,1]{2,1,0:T(1,128)} %broadcast_in_dim.145), calls=%async_computation | async-start | bytes 65536 | tf_op jit(solution)/shard_map/all_to_all | solution.py:11
  45.2 20.9 %all_to_all.67 = f32[64,1,8,512]{3,2,1,0:T(8,128)S(1)} all-to-all(f32[64,1,8,512]{3,2,1,0:T(8,128)S(1)} %get-tuple-element.163), channel_id=1, replica_groups=mesh['rows'=2,'cols'=64] {'cols'}, dimensions={0} | all-to-all | bytes 2097152 | tf_op jit(solution)/shard_map/all_to_all | solution.py:160
  75.9 10.3 %all-to-all-done.3 = f32[64,1,8,512]{3,2,1,0:T(8,128)S(1)} async-done(((f32[64,1,8,512]{3,2,1,0:T(8,128)}), f32[64,1,8,512]{3,2,1,0:T(8,128)S(1)}, u32[]{:S(2)}, u32[]{:S(2)}) %all-to-all-start.3) | async-done | bytes 1048608 | tf_op jit(solution)/shard_map/all_to_all | solution.py:161
  90.9 208.2 %while.12 = (s32[]{:T(128)}, f32[3,2,2,64,1024]{4,3,2,1,0:T(8,128)}, s32[3,2]{1,0:T(4,128)S(1)}, s32[3,2]{1,0:T(4,128)S(1)}, f32[3,2,8,1024]{3,2,1,0:T(8,128)S(1...) while((s32[]{:T(128)}, f32[3,2,2,64,1024]{4,3,2,1,0:T(8,128)}, ...), condition=%wide.region_5.6_spmd, body=%wide.region_1.5_spmd.sunk | while | flops 3671470336 | bytes 37377732 | solution.py:124
  92.0 21.5 %fusion.96 = f32[2,1024,64]{1,2,0:T(8,128)S(1)} fusion(f32[2,1024]{1,0:T(2,128)S(1)} %get-tuple-element.239, f32[2,1024]{1,0:T(2,128)S(1)} %get-tuple-element.241, f32[2,1024]{1,0:T(2,128)S(1)} %get-tuple-element.242, f32[2,1024]{1,0:T(2,128)S(1)} %get-tuple-element.243, f32[2,1024]{1,0:T(2,128)S(1)} %get-tuple-element.244, ...), kind=kOutput, calls=%fused_computation.40.clone.1 | convolution fusion | flops 1684013056 | bytes 5103624 | tf_op jit(solution)/shard_map/while/body/eval_jaxpr/gik,kr->gir/dot_general | solution.py:111
  114.4 11.7 %custom-call.42 = f32[2,64,64]{2,1,0:T(8,128)S(1)} custom-call(f32[2,64,64]{2,1,0:T(8,128)S(1)} %fusion.99), custom_call_target="Cholesky" | custom-call | tf_op jit(solution)/shard_map/while/body/eval_jaxpr/jit(cholesky)/cholesky | solution.py:72
  126.4 10.0 %custom-call.43 = f32[2,1,64,64]{2,3,1,0:T(8,128)S(1)} custom-call(f32[2,1,64,64]{3,2,1,0:T(8,128)S(1)} %select_bitcast_fusion.3), custom_call_target="InvertDiagBlocksLowerTriangular" | custom-call | tf_op jit(solution)/shard_map/while/body/eval_jaxpr/triangular_solve | solution.py:74
  136.4 20.7 %fusion.97 = f32[2,64,1024]{2,1,0:T(8,128)S(1)} fusion(f32[2,1024,64]{1,2,0:T(8,128)S(1)} %fusion.96, f32[2,1024]{1,0:T(2,128)S(1)} %get-tuple-element.239, f32[2,1024]{1,0:T(2,128)S(1)} %get-tuple-element.241, f32[2,1024]{1,0:T(2,128)S(1)} %get-tuple-element.242, f32[2,1024]{1,0:T(2,128)S(1)} %get-tuple-element.243, ...), kind=kOutput, calls=%fused_computation.39.clone.1 | convolution fusion | flops 1684013056 | bytes 5365768 | tf_op jit(solution)/shard_map/while/body/eval_jaxpr/gik,gir->grk/dot_general | solution.py:113
  160.5 21.1 %fusion.96 = f32[2,1024,64]{1,2,0:T(8,128)S(1)} fusion(f32[2,1024]{1,0:T(2,128)S(1)} %get-tuple-element.239, f32[2,1024]{1,0:T(2,128)S(1)} %get-tuple-element.241, f32[2,1024]{1,0:T(2,128)S(1)} %get-tuple-element.242, f32[2,1024]{1,0:T(2,128)S(1)} %get-tuple-element.243, f32[2,1024]{1,0:T(2,128)S(1)} %get-tuple-element.244, ...), kind=kOutput, calls=%fused_computation.40.clone.1 | convolution fusion | flops 1684013056 | bytes 5103624 | tf_op jit(solution)/shard_map/while/body/eval_jaxpr/gik,kr->gir/dot_general | solution.py:111
  182.5 11.7 %custom-call.42 = f32[2,64,64]{2,1,0:T(8,128)S(1)} custom-call(f32[2,64,64]{2,1,0:T(8,128)S(1)} %fusion.99), custom_call_target="Cholesky" | custom-call | tf_op jit(solution)/shard_map/while/body/eval_jaxpr/jit(cholesky)/cholesky | solution.py:72
  194.5 10.0 %custom-call.43 = f32[2,1,64,64]{2,3,1,0:T(8,128)S(1)} custom-call(f32[2,1,64,64]{3,2,1,0:T(8,128)S(1)} %select_bitcast_fusion.3), custom_call_target="InvertDiagBlocksLowerTriangular" | custom-call | tf_op jit(solution)/shard_map/while/body/eval_jaxpr/triangular_solve | solution.py:74
  204.6 20.8 %fusion.97 = f32[2,64,1024]{2,1,0:T(8,128)S(1)} fusion(f32[2,1024,64]{1,2,0:T(8,128)S(1)} %fusion.96, f32[2,1024]{1,0:T(2,128)S(1)} %get-tuple-element.239, f32[2,1024]{1,0:T(2,128)S(1)} %get-tuple-element.241, f32[2,1024]{1,0:T(2,128)S(1)} %get-tuple-element.242, f32[2,1024]{1,0:T(2,128)S(1)} %get-tuple-element.243, ...), kind=kOutput, calls=%fused_computation.39.clone.1 | convolution fusion | flops 1684013056 | bytes 5365768 | tf_op jit(solution)/shard_map/while/body/eval_jaxpr/gik,gir->grk/dot_general | solution.py:113
  228.6 21.1 %fusion.96 = f32[2,1024,64]{1,2,0:T(8,128)S(1)} fusion(f32[2,1024]{1,0:T(2,128)S(1)} %get-tuple-element.239, f32[2,1024]{1,0:T(2,128)S(1)} %get-tuple-element.241, f32[2,1024]{1,0:T(2,128)S(1)} %get-tuple-element.242, f32[2,1024]{1,0:T(2,128)S(1)} %get-tuple-element.243, f32[2,1024]{1,0:T(2,128)S(1)} %get-tuple-element.244, ...), kind=kOutput, calls=%fused_computation.40.clone.1 | convolution fusion | flops 1684013056 | bytes 5103624 | tf_op jit(solution)/shard_map/while/body/eval_jaxpr/gik,kr->gir/dot_general | solution.py:111
  250.7 11.7 %custom-call.42 = f32[2,64,64]{2,1,0:T(8,128)S(1)} custom-call(f32[2,64,64]{2,1,0:T(8,128)S(1)} %fusion.99), custom_call_target="Cholesky" | custom-call | tf_op jit(solution)/shard_map/while/body/eval_jaxpr/jit(cholesky)/cholesky | solution.py:72
  262.7 10.2 %custom-call.43 = f32[2,1,64,64]{2,3,1,0:T(8,128)S(1)} custom-call(f32[2,1,64,64]{3,2,1,0:T(8,128)S(1)} %select_bitcast_fusion.3), custom_call_target="InvertDiagBlocksLowerTriangular" | custom-call | tf_op jit(solution)/shard_map/while/body/eval_jaxpr/triangular_solve | solution.py:74
  272.9 20.6 %fusion.97 = f32[2,64,1024]{2,1,0:T(8,128)S(1)} fusion(f32[2,1024,64]{1,2,0:T(8,128)S(1)} %fusion.96, f32[2,1024]{1,0:T(2,128)S(1)} %get-tuple-element.239, f32[2,1024]{1,0:T(2,128)S(1)} %get-tuple-element.241, f32[2,1024]{1,0:T(2,128)S(1)} %get-tuple-element.242, f32[2,1024]{1,0:T(2,128)S(1)} %get-tuple-element.243, ...), kind=kOutput, calls=%fused_computation.39.clone.1 | convolution fusion | flops 1684013056 | bytes 5365768 | tf_op jit(solution)/shard_map/while/body/eval_jaxpr/gik,gir->grk/dot_general | solution.py:113
  308.5 9.6 %reshape.618 = f32[2,1,393216]{2,1,0:T(1,128)} reshape(f32[1024,1,6,2,64]{4,3,2,1,0:T(2,128)} %bitcast.201) | data formatting | bytes 6291456
  318.1 10.8 %all_to_all.69 = f32[2,1,393216]{2,1,0:T(1,128)} all-to-all(f32[2,1,393216]{2,1,0:T(1,128)} %reshape.618), channel_id=1, replica_groups=mesh['rows'=2,'cols'=64] {'rows'}, dimensions={0} | all-to-all | bytes 6291456 | tf_op jit(solution)/shard_map/all_to_all | solution.py:126
  329.4 12.6 %reduce.17 = f32[2,393216]{1,0:T(2,128)} reduce(f32[2,1,393216]{2,1,0:T(1,128)} %all_to_all.69, f32[]{:T(128)} %broadcast.1032), dimensions={1}, to_apply=%all_to_all.54.reduce_sub_computation | reduce | bytes 6291460 | tf_op jit(solution)/shard_map/all_to_all | solution.py:126
  342.0 10.4 %reshape.619 = f32[1024,1,6,2,64]{4,3,2,1,0:T(2,128)} reshape(f32[2,393216]{1,0:T(2,128)} %reduce.17) | data formatting | bytes 6291456
  376.1 9.4 %fusion.41 = (f32[64,1,64,512]{3,2,1,0:T(8,128)}, f32[64,1,64,512]{3,2,1,0:T(8,128)S(1)}) fusion(f32[64,64,512]{2,1,0:T(8,128)} %gather_fusion.10, pred[64]{0:T(512)(128)(4,1)S(1)} %copy-done.3, f32[64,64,512]{2,1,0:T(8,128)} %gather_fusion.8), kind=kLoop, calls=%fused_computation.95 | loop fusion | flops 4194304 | bytes 33554496 | tf_op jit(solution)/shard_map/jit(_where)/select_n | solution.py:182
  385.5 102.9 %all_to_all.70 = f32[64,1,64,512]{3,2,1,0:T(8,128)} all-to-all(f32[64,1,64,512]{3,2,1,0:T(8,128)S(1)} %get-tuple-element.162), channel_id=1, replica_groups=mesh['rows'=2,'cols'=64] {'cols'}, dimensions={0} | all-to-all | bytes 16777216 | tf_op jit(solution)/shard_map/all_to_all | solution.py:186
  503.4 111.5 %all-to-all-done.7 = f32[64,1,64,512]{3,2,1,0:T(8,128)} async-done(((f32[64,1,64,512]{3,2,1,0:T(8,128)}), f32[64,1,64,512]{3,2,1,0:T(8,128)}, u32[]{:S(2)}, u32[]{:S(2)}) %all-to-all-start.7) | async-done | bytes 8388640 | tf_op jit(solution)/shard_map/all_to_all | solution.py:187
  622.0 12.4 %broadcast_select_fusion = (f32[48,64,512]{2,1,0:T(8,128)}, f32[48,64,512]{2,1,0:T(8,128)}) fusion(f32[48,64,512]{2,1,0:T(8,128)} %gather_fusion.11, pred[48]{0:T(512)(128)(4,1)S(1)} %iota_compare_fusion.4, f32[48,64,512]{2,1,0:T(8,128)} %gather_fusion.9), kind=kLoop, calls=%fused_computation.98 | loop fusion | flops 3145728 | bytes 25165872 | tf_op jit(solution)/shard_map/jit(_where)/select_n | solution.py:193
  (146 shorter events, 113.5 us)
Async XLA Ops:
  0.6 35.2 %copy-start = (f32[48,8,512]{2,1,0:T(8,128)S(1)}, f32[48,8,512]{2,1,0:T(8,128)}, u32[]{:S(2)}) copy-start(f32[48,8,512]{2,1,0:T(8,128)} %param.8) | copy-start | bytes 2359300
  2.0 19.0 %all-to-all-start = ((s32[64,1,1]{2,1,0:T(1,128)}), s32[64,1,1]{2,1,0:T(1,128)S(1)}, u32[]{:S(2)}, u32[]{:S(2)}) async-start(s32[64,1,1]{2,1,0:T(1,128)} %broadcast_in_dim.145), calls=%async_computation | async-start | bytes 65536 | tf_op jit(solution)/shard_map/all_to_all | solution.py:11
  28.9 14.4 %all-to-all-start.1 = ((f32[64,1,3]{2,1,0:T(1,128)}), f32[64,1,3]{2,1,0:T(1,128)S(1)}, u32[]{:S(2)}, u32[]{:S(2)}) async-start(f32[64,1,3]{2,1,0:T(1,128)} %copy.46), calls=%async_computation.1 | async-start | bytes 65536 | tf_op jit(solution)/shard_map/all_to_all | solution.py:162
  36.5 54.5 %copy-start.4 = (f32[1024,64]{0,1:T(8,128)S(1)}, f32[1024,64]{0,1:T(8,128)}, u32[]{:S(2)}) copy-start(f32[1024,64]{0,1:T(8,128)} %param.13) | copy-start | bytes 786436
  66.1 20.0 %all-to-all-start.3 = ((f32[64,1,8,512]{3,2,1,0:T(8,128)}), f32[64,1,8,512]{3,2,1,0:T(8,128)S(1)}, u32[]{:S(2)}, u32[]{:S(2)}) async-start(f32[64,1,8,512]{3,2,1,0:T(8,128)} %get-tuple-element.164), calls=%async_computation.3 | async-start | bytes 2097152 | tf_op jit(solution)/shard_map/all_to_all | solution.py:161
  92.0 21.5 %copy-start.2 = (s32[1024,1024]{1,0:T(8,128)}, s32[1024,1024]{1,0:T(8,128)S(1)}, u32[]{:S(2)}) copy-start(s32[1024,1024]{1,0:T(8,128)S(1)} %iota_subtract_fusion.2) | copy-start | bytes 12582916 | tf_op jit(solution)/shard_map/while
  160.5 21.1 %copy-start.2 = (s32[1024,1024]{1,0:T(8,128)}, s32[1024,1024]{1,0:T(8,128)S(1)}, u32[]{:S(2)}) copy-start(s32[1024,1024]{1,0:T(8,128)S(1)} %iota_subtract_fusion.2) | copy-start | bytes 12582916 | tf_op jit(solution)/shard_map/while
  228.6 21.2 %copy-start.2 = (s32[1024,1024]{1,0:T(8,128)}, s32[1024,1024]{1,0:T(8,128)S(1)}, u32[]{:S(2)}) copy-start(s32[1024,1024]{1,0:T(8,128)S(1)} %iota_subtract_fusion.2) | copy-start | bytes 12582916 | tf_op jit(solution)/shard_map/while
  371.5 4.6 copy-start.3
  488.4 126.5 %all-to-all-start.7 = ((f32[64,1,64,512]{3,2,1,0:T(8,128)}), f32[64,1,64,512]{3,2,1,0:T(8,128)}, u32[]{:S(2)}, u32[]{:S(2)}) async-start(f32[64,1,64,512]{3,2,1,0:T(8,128)} %get-tuple-element.161), calls=%async_computation.7 | async-start | bytes 16777216 | tf_op jit(solution)/shard_map/all_to_all | solution.py:187
  614.9 19.5 %copy-start.1 = (f32[48,8,512]{2,1,0:T(8,128)S(1)}, f32[48,8,512]{2,1,0:T(8,128)}, u32[]{:S(2)}) copy-start(f32[48,8,512]{2,1,0:T(8,128)} %param.8) | copy-start | bytes 2359300
where the time goes:
time: 641 us; the launch traced here: 635 us
  blocking collectives  139 us (22%)
  waiting for transfers between devices  134 us (21%)
  matrix products  131 us (20%)
  other arithmetic  110 us (17%)
  local copies, waits for them, and re-layouts  80 us (12%)
  starting transfers between devices  32.7 us (5%)
    all_to_all x1, waiting for transfers between devices, on_device(): lax.all_to_all(back_right, 'cols', split_axis=0, concat_axis=0, tiled=True)  112 us
    all_to_all x1, blocking collectives, on_device(): lax.all_to_all(back_left, 'cols', split_axis=0, concat_axis=0, tiled=True)  103 us
    dot_general x3, matrix products, step(): sketched = jnp.einsum('gik,kr->gir', block, sketch, precision=HIGHEST)  63.7 us
    dot_general x3, matrix products, step(): projected = jnp.einsum('gik,gir->grk', block, sketched, precision=HIGHEST)  62.1 us
    another operation x12, other arithmetic, factor_pair(): lower = jnp.linalg.cholesky(system)  35.7 us
    another operation x9, other arithmetic, factor_pair(): lax.linalg.triangular_solve(lower, half, left_side=True, lower=True, tran...  30.5 us
    all_to_all x1, blocking collectives, on_device(): lax.all_to_all(send_rows, 'cols', split_axis=0, concat_axis=0, tiled=True)  20.9 us
    unnamed x10, local copies, waits for them, and re-layouts  20 us
  transfers between devices with their start and end apart: 4, of which 4 were waited for; matrix products, arithmetic and copies ran while one was open for 2% of the time, Pallas kernels for 0%

commit v1 on v0

--- a/solution.py
+++ b/solution.py
@@ -123,7 +123,10 @@
     )
     results = lax.scan(step, jnp.int32(0), packed)[1]
     results = results.reshape(turns, 1, 2, rank, full_width)
-    returned = lax.all_to_all(results, "rows", split_axis=4, concat_axis=1, tiled=True)
+    returned = jnp.concatenate(
+        lax.all_to_all(jnp.stack(jnp.split(results, lax.axis_size("rows"), axis=4)), "rows", 0, 0),
+        axis=1,
+    )
     flat = returned.reshape(slots, 2, rank, width)
     return (flat[:, 0], flat[:, 1])
 

time: 641 us -> 588 us (0.917)
  local copies, waits for them, and re-layouts: 80 us -> 40.9 us
  other arithmetic: 110 us -> 97.6 us
    unnamed x10 -> x8, local copies, waits for them, and re-layouts: 20 us -> 0.03 us
    all_to_all x1 -> x0, other arithmetic: 12.6 us -> none  [whole_compress(): lax.all_to_all(results, 'rows', split_axis=4, concat_axis=1, tiled=True)]
    all_to_all x3 -> x0, local copies, waits for them, and re-layouts: 12.4 us -> none  [whole_compress(): lax.all_to_all(results, 'rows', split_axis=4, concat_axis=1, tiled=True)]
    reshape x1, local copies, waits for them, and re-layouts: 9.42 us -> 0.46 us  [whole_compress(): jnp.concatenate(lax.all_to_all(jnp.stack(jnp.split(results, lax.axis_size...]
where the time goes in v1:
time: 588 us; the launch traced here: 582 us
  waiting for transfers between devices  134 us (23%)
  blocking collectives  134 us (23%)
  matrix products  131 us (22%)
  other arithmetic  97.6 us (17%)
  local copies, waits for them, and re-layouts  40.9 us (7%)
  starting transfers between devices  32.7 us (6%)
  loops' own time  7.75 us (1%)
    all_to_all x1, waiting for transfers between devices, on_device(): lax.all_to_all(back_right, 'cols', split_axis=0, concat_axis=0, tiled=True)  112 us
    all_to_all x1, blocking collectives, on_device(): lax.all_to_all(back_left, 'cols', split_axis=0, concat_axis=0, tiled=True)  103 us
    dot_general x3, matrix products, step(): sketched = jnp.einsum('gik,kr->gir', block, sketch, precision=HIGHEST)  63.6 us
    dot_general x3, matrix products, step(): projected = jnp.einsum('gik,gir->grk', block, sketched, precision=HIGHEST)  62.1 us
    another operation x12, other arithmetic, factor_pair(): lower = jnp.linalg.cholesky(system)  35.7 us
    another operation x9, other arithmetic, factor_pair(): lax.linalg.triangular_solve(lower, half, left_side=True, lower=True, tran...  30.5 us
    all_to_all x1, blocking collectives, on_device(): lax.all_to_all(send_rows, 'cols', split_axis=0, concat_axis=0, tiled=True)  20.9 us
    select_n x1, other arithmetic, on_device(): return (jnp.where(is_kept, left, 0.0), jnp.where(is_kept, right, 0.0))  12.4 us
  transfers between devices with their start and end apart: 4, of which 4 were waited for; matrix products, arithmetic and copies ran while one was open for 2% of the time, Pallas kernels for 0%

profile of v1, /device:TPU:4, one launch (start us, length us, event | category | flops | bytes accessed | tf_op | source)
XLA Modules:
  0.0 582.0 jit_solution(8813023206905552363)
XLA Ops:
  2.0 11.5 %all-to-all-start = ((s32[64,1,1]{2,1,0:T(1,128)}), s32[64,1,1]{2,1,0:T(1,128)S(1)}, u32[]{:S(2)}, u32[]{:S(2)}) async-start(s32[64,1,1]{2,1,0:T(1,128)} %broadcast_in_dim.145), calls=%async_computation | async-start | bytes 65536 | tf_op jit(solution)/shard_map/all_to_all | solution.py:11
  13.5 7.5 %all-to-all-done = s32[64,1,1]{2,1,0:T(1,128)S(1)} async-done(((s32[64,1,1]{2,1,0:T(1,128)}), s32[64,1,1]{2,1,0:T(1,128)S(1)}, u32[]{:S(2)}, u32[]{:S(2)}) %all-to-all-start) | async-done | bytes 288 | tf_op jit(solution)/shard_map/all_to_all | solution.py:11
  45.2 20.9 %all_to_all.57 = f32[64,1,8,512]{3,2,1,0:T(8,128)S(1)} all-to-all(f32[64,1,8,512]{3,2,1,0:T(8,128)S(1)} %get-tuple-element.165), channel_id=1, replica_groups=mesh['rows'=2,'cols'=64] {'cols'}, dimensions={0} | all-to-all | bytes 2097152 | tf_op jit(solution)/shard_map/all_to_all | solution.py:163
  75.9 10.3 %all-to-all-done.3 = f32[64,1,8,512]{3,2,1,0:T(8,128)S(1)} async-done(((f32[64,1,8,512]{3,2,1,0:T(8,128)}), f32[64,1,8,512]{3,2,1,0:T(8,128)S(1)}, u32[]{:S(2)}, u32[]{:S(2)}) %all-to-all-start.3) | async-done | bytes 1048608 | tf_op jit(solution)/shard_map/all_to_all | solution.py:164
  90.9 211.2 %while.12 = (s32[]{:T(128)}, f32[3,2,2,64,1024]{4,3,2,1,0:T(8,128)}, s32[3,2]{1,0:T(4,128)S(1)}, s32[3,2]{1,0:T(4,128)S(1)}, f32[3,2,8,1024]{3,2,1,0:T(8,128)S(1...) while((s32[]{:T(128)}, f32[3,2,2,64,1024]{4,3,2,1,0:T(8,128)}, ...), condition=%wide.region_5.6_spmd, body=%wide.region_1.5_spmd.sunk | while | flops 3671470336 | bytes 37377732 | solution.py:124
  92.1 21.3 %fusion.96 = f32[2,1024,64]{1,2,0:T(8,128)S(1)} fusion(f32[2,1024]{1,0:T(2,128)S(1)} %get-tuple-element.241, f32[2,1024]{1,0:T(2,128)S(1)} %get-tuple-element.243, f32[2,1024]{1,0:T(2,128)S(1)} %get-tuple-element.244, f32[2,1024]{1,0:T(2,128)S(1)} %get-tuple-element.245, f32[2,1024]{1,0:T(2,128)S(1)} %get-tuple-element.246, ...), kind=kOutput, calls=%fused_computation.40.clone.1 | convolution fusion | flops 1684013056 | bytes 5103624 | tf_op jit(solution)/shard_map/while/body/eval_jaxpr/gik,kr->gir/dot_general | solution.py:111
  114.4 11.7 %custom-call.42 = f32[2,64,64]{2,1,0:T(8,128)S(1)} custom-call(f32[2,64,64]{2,1,0:T(8,128)S(1)} %fusion.99), custom_call_target="Cholesky" | custom-call | tf_op jit(solution)/shard_map/while/body/eval_jaxpr/jit(cholesky)/cholesky | solution.py:72
  126.4 10.0 %custom-call.43 = f32[2,1,64,64]{2,3,1,0:T(8,128)S(1)} custom-call(f32[2,1,64,64]{3,2,1,0:T(8,128)S(1)} %select_bitcast_fusion.3), custom_call_target="InvertDiagBlocksLowerTriangular" | custom-call | tf_op jit(solution)/shard_map/while/body/eval_jaxpr/triangular_solve | solution.py:74
  136.4 20.7 %fusion.97 = f32[2,64,1024]{2,1,0:T(8,128)S(1)} fusion(f32[2,1024,64]{1,2,0:T(8,128)S(1)} %fusion.96, f32[2,1024]{1,0:T(2,128)S(1)} %get-tuple-element.241, f32[2,1024]{1,0:T(2,128)S(1)} %get-tuple-element.243, f32[2,1024]{1,0:T(2,128)S(1)} %get-tuple-element.244, f32[2,1024]{1,0:T(2,128)S(1)} %get-tuple-element.245, ...), kind=kOutput, calls=%fused_computation.39.clone.1 | convolution fusion | flops 1684013056 | bytes 5365768 | tf_op jit(solution)/shard_map/while/body/eval_jaxpr/gik,gir->grk/dot_general | solution.py:113
  160.5 21.1 %fusion.96 = f32[2,1024,64]{1,2,0:T(8,128)S(1)} fusion(f32[2,1024]{1,0:T(2,128)S(1)} %get-tuple-element.241, f32[2,1024]{1,0:T(2,128)S(1)} %get-tuple-element.243, f32[2,1024]{1,0:T(2,128)S(1)} %get-tuple-element.244, f32[2,1024]{1,0:T(2,128)S(1)} %get-tuple-element.245, f32[2,1024]{1,0:T(2,128)S(1)} %get-tuple-element.246, ...), kind=kOutput, calls=%fused_computation.40.clone.1 | convolution fusion | flops 1684013056 | bytes 5103624 | tf_op jit(solution)/shard_map/while/body/eval_jaxpr/gik,kr->gir/dot_general | solution.py:111
  182.5 11.7 %custom-call.42 = f32[2,64,64]{2,1,0:T(8,128)S(1)} custom-call(f32[2,64,64]{2,1,0:T(8,128)S(1)} %fusion.99), custom_call_target="Cholesky" | custom-call | tf_op jit(solution)/shard_map/while/body/eval_jaxpr/jit(cholesky)/cholesky | solution.py:72
  194.5 10.0 %custom-call.43 = f32[2,1,64,64]{2,3,1,0:T(8,128)S(1)} custom-call(f32[2,1,64,64]{3,2,1,0:T(8,128)S(1)} %select_bitcast_fusion.3), custom_call_target="InvertDiagBlocksLowerTriangular" | custom-call | tf_op jit(solution)/shard_map/while/body/eval_jaxpr/triangular_solve | solution.py:74
  204.5 20.8 %fusion.97 = f32[2,64,1024]{2,1,0:T(8,128)S(1)} fusion(f32[2,1024,64]{1,2,0:T(8,128)S(1)} %fusion.96, f32[2,1024]{1,0:T(2,128)S(1)} %get-tuple-element.241, f32[2,1024]{1,0:T(2,128)S(1)} %get-tuple-element.243, f32[2,1024]{1,0:T(2,128)S(1)} %get-tuple-element.244, f32[2,1024]{1,0:T(2,128)S(1)} %get-tuple-element.245, ...), kind=kOutput, calls=%fused_computation.39.clone.1 | convolution fusion | flops 1684013056 | bytes 5365768 | tf_op jit(solution)/shard_map/while/body/eval_jaxpr/gik,gir->grk/dot_general | solution.py:113
  228.6 21.1 %fusion.96 = f32[2,1024,64]{1,2,0:T(8,128)S(1)} fusion(f32[2,1024]{1,0:T(2,128)S(1)} %get-tuple-element.241, f32[2,1024]{1,0:T(2,128)S(1)} %get-tuple-element.243, f32[2,1024]{1,0:T(2,128)S(1)} %get-tuple-element.244, f32[2,1024]{1,0:T(2,128)S(1)} %get-tuple-element.245, f32[2,1024]{1,0:T(2,128)S(1)} %get-tuple-element.246, ...), kind=kOutput, calls=%fused_computation.40.clone.1 | convolution fusion | flops 1684013056 | bytes 5103624 | tf_op jit(solution)/shard_map/while/body/eval_jaxpr/gik,kr->gir/dot_general | solution.py:111
  250.7 11.7 %custom-call.42 = f32[2,64,64]{2,1,0:T(8,128)S(1)} custom-call(f32[2,64,64]{2,1,0:T(8,128)S(1)} %fusion.99), custom_call_target="Cholesky" | custom-call | tf_op jit(solution)/shard_map/while/body/eval_jaxpr/jit(cholesky)/cholesky | solution.py:72
  262.7 10.2 %custom-call.43 = f32[2,1,64,64]{2,3,1,0:T(8,128)S(1)} custom-call(f32[2,1,64,64]{3,2,1,0:T(8,128)S(1)} %select_bitcast_fusion.3), custom_call_target="InvertDiagBlocksLowerTriangular" | custom-call | tf_op jit(solution)/shard_map/while/body/eval_jaxpr/triangular_solve | solution.py:74
  272.9 20.6 %fusion.97 = f32[2,64,1024]{2,1,0:T(8,128)S(1)} fusion(f32[2,1024,64]{1,2,0:T(8,128)S(1)} %fusion.96, f32[2,1024]{1,0:T(2,128)S(1)} %get-tuple-element.241, f32[2,1024]{1,0:T(2,128)S(1)} %get-tuple-element.243, f32[2,1024]{1,0:T(2,128)S(1)} %get-tuple-element.244, f32[2,1024]{1,0:T(2,128)S(1)} %get-tuple-element.245, ...), kind=kOutput, calls=%fused_computation.39.clone.1 | convolution fusion | flops 1684013056 | bytes 5365768 | tf_op jit(solution)/shard_map/while/body/eval_jaxpr/gik,gir->grk/dot_general | solution.py:113
  323.5 9.3 %fusion.41 = (f32[64,1,64,512]{3,2,1,0:T(8,128)}, f32[64,1,64,512]{3,2,1,0:T(8,128)S(1)}) fusion(f32[64,64,512]{2,1,0:T(8,128)} %gather_fusion.10, pred[64]{0:T(512)(128)(4,1)S(1)} %copy-done.3, f32[64,64,512]{2,1,0:T(8,128)} %gather_fusion.8), kind=kLoop, calls=%fused_computation.95 | loop fusion | flops 4194304 | bytes 33554496 | tf_op jit(solution)/shard_map/jit(_where)/select_n | solution.py:185
  332.8 102.9 %all_to_all.60 = f32[64,1,64,512]{3,2,1,0:T(8,128)} all-to-all(f32[64,1,64,512]{3,2,1,0:T(8,128)S(1)} %get-tuple-element.164), channel_id=1, replica_groups=mesh['rows'=2,'cols'=64] {'cols'}, dimensions={0} | all-to-all | bytes 16777216 | tf_op jit(solution)/shard_map/all_to_all | solution.py:189
  435.7 7.9 %all-to-all-start.7 = ((f32[64,1,64,512]{3,2,1,0:T(8,128)}), f32[64,1,64,512]{3,2,1,0:T(8,128)}, u32[]{:S(2)}, u32[]{:S(2)}) async-start(f32[64,1,64,512]{3,2,1,0:T(8,128)} %get-tuple-element.163), calls=%async_computation.7 | async-start | bytes 16777216 | tf_op jit(solution)/shard_map/all_to_all | solution.py:190
  443.6 7.0 %gather_fusion.9 = f32[48,64,512]{2,1,0:T(8,128)} fusion(f32[64,64,512]{2,1,0:T(8,128)} %bitcast.201, s32[1024]{0:T(1024)S(1)} %pad_clamp_fusion), kind=kCustom, calls=%fused_computation.9 | custom fusion | bytes 12583104 | tf_op jit(solution)/shard_map/gather | solution.py:193
  450.7 111.5 %all-to-all-done.7 = f32[64,1,64,512]{3,2,1,0:T(8,128)} async-done(((f32[64,1,64,512]{3,2,1,0:T(8,128)}), f32[64,1,64,512]{3,2,1,0:T(8,128)}, u32[]{:S(2)}, u32[]{:S(2)}) %all-to-all-start.7) | async-done | bytes 8388640 | tf_op jit(solution)/shard_map/all_to_all | solution.py:190
  562.2 7.1 %gather_fusion.11 = f32[48,64,512]{2,1,0:T(8,128)} fusion(f32[64,64,512]{2,1,0:T(8,128)} %bitcast.64, s32[1024]{0:T(1024)S(1)} %pad_clamp_fusion), kind=kCustom, calls=%fused_computation.11 | custom fusion | bytes 12583104 | tf_op jit(solution)/shard_map/gather | solution.py:194
  569.3 12.4 %broadcast_select_fusion = (f32[48,64,512]{2,1,0:T(8,128)}, f32[48,64,512]{2,1,0:T(8,128)}) fusion(f32[48,64,512]{2,1,0:T(8,128)} %gather_fusion.11, pred[48]{0:T(512)(128)(4,1)S(1)} %iota_compare_fusion.4, f32[48,64,512]{2,1,0:T(8,128)} %gather_fusion.9), kind=kLoop, calls=%fused_computation.99 | loop fusion | flops 3145728 | bytes 25165872 | tf_op jit(solution)/shard_map/jit(_where)/select_n | solution.py:196
  (142 shorter events, 71.5 us)
Async XLA Ops:
  0.6 35.2 %copy-start = (f32[48,8,512]{2,1,0:T(8,128)S(1)}, f32[48,8,512]{2,1,0:T(8,128)}, u32[]{:S(2)}) copy-start(f32[48,8,512]{2,1,0:T(8,128)} %param.8) | copy-start | bytes 2359300
  2.0 19.0 %all-to-all-start = ((s32[64,1,1]{2,1,0:T(1,128)}), s32[64,1,1]{2,1,0:T(1,128)S(1)}, u32[]{:S(2)}, u32[]{:S(2)}) async-start(s32[64,1,1]{2,1,0:T(1,128)} %broadcast_in_dim.145), calls=%async_computation | async-start | bytes 65536 | tf_op jit(solution)/shard_map/all_to_all | solution.py:11
  28.9 14.4 %all-to-all-start.1 = ((f32[64,1,3]{2,1,0:T(1,128)}), f32[64,1,3]{2,1,0:T(1,128)S(1)}, u32[]{:S(2)}, u32[]{:S(2)}) async-start(f32[64,1,3]{2,1,0:T(1,128)} %copy.45), calls=%async_computation.1 | async-start | bytes 65536 | tf_op jit(solution)/shard_map/all_to_all | solution.py:165
  36.5 54.5 %copy-start.4 = (f32[1024,64]{0,1:T(8,128)S(1)}, f32[1024,64]{0,1:T(8,128)}, u32[]{:S(2)}) copy-start(f32[1024,64]{0,1:T(8,128)} %param.13) | copy-start | bytes 786436
  66.1 20.0 %all-to-all-start.3 = ((f32[64,1,8,512]{3,2,1,0:T(8,128)}), f32[64,1,8,512]{3,2,1,0:T(8,128)S(1)}, u32[]{:S(2)}, u32[]{:S(2)}) async-start(f32[64,1,8,512]{3,2,1,0:T(8,128)} %get-tuple-element.166), calls=%async_computation.3 | async-start | bytes 2097152 | tf_op jit(solution)/shard_map/all_to_all | solution.py:164
  92.1 21.3 %copy-start.2 = (s32[1024,1024]{1,0:T(8,128)}, s32[1024,1024]{1,0:T(8,128)S(1)}, u32[]{:S(2)}) copy-start(s32[1024,1024]{1,0:T(8,128)S(1)} %iota_subtract_fusion.2) | copy-start | bytes 12582916 | tf_op jit(solution)/shard_map/while
  160.5 21.1 %copy-start.2 = (s32[1024,1024]{1,0:T(8,128)}, s32[1024,1024]{1,0:T(8,128)S(1)}, u32[]{:S(2)}) copy-start(s32[1024,1024]{1,0:T(8,128)S(1)} %iota_subtract_fusion.2) | copy-start | bytes 12582916 | tf_op jit(solution)/shard_map/while
  228.6 21.2 %copy-start.2 = (s32[1024,1024]{1,0:T(8,128)}, s32[1024,1024]{1,0:T(8,128)S(1)}, u32[]{:S(2)}) copy-start(s32[1024,1024]{1,0:T(8,128)S(1)} %iota_subtract_fusion.2) | copy-start | bytes 12582916 | tf_op jit(solution)/shard_map/while
  318.9 4.6 copy-start.3
  435.7 126.5 %all-to-all-start.7 = ((f32[64,1,64,512]{3,2,1,0:T(8,128)}), f32[64,1,64,512]{3,2,1,0:T(8,128)}, u32[]{:S(2)}, u32[]{:S(2)}) async-start(f32[64,1,64,512]{3,2,1,0:T(8,128)} %get-tuple-element.163), calls=%async_computation.7 | async-start | bytes 16777216 | tf_op jit(solution)/shard_map/all_to_all | solution.py:190
  562.2 19.5 %copy-start.1 = (f32[48,8,512]{2,1,0:T(8,128)S(1)}, f32[48,8,512]{2,1,0:T(8,128)}, u32[]{:S(2)}) copy-start(f32[48,8,512]{2,1,0:T(8,128)} %param.8) | copy-start | bytes 2359300
